TPU v7x, 128 devices: a whole 4x4x4 slice. The times are simulated.
128 devices in a mesh: leaf: 32 (over y, z, core), sub: 4 (over x).
Axes of the slice: x: 4, y: 4, z: 4, core: 2. Of those that a mesh axis runs over, the one named last changes fastest.
Arguments:
- points: float32 [8192, 8, 128], P(('leaf', 'sub')), may hold values from -6 to 6
- probes: bfloat16 [8192, 32, 128], P(('leaf', 'sub')), may hold values from -6 to 6
- leaf_basis: bfloat16 [8192, 64, 128], P(('leaf', 'sub')), may hold values from -0.5 to 0.5
- mid_transfer: float32 [8192, 64, 64], P(('leaf', 'sub')), may hold values from -0.25 to 0.25
- top_transfer: float32 [1024, 64, 64], P(('leaf', 'sub')), may hold values from -0.25 to 0.25
- mid_skeleton: float32 [1024, 8, 64], P(('leaf', 'sub')), may hold values from -6 to 6
- top_skeleton: float32 [32, 8, 64], replicated, may hold values from -6 to 6
- near_list: int32 [8192, 8], P(('leaf', 'sub')), may hold values from -1 to 8191, as said below
- mid_list: int32 [1024, 6], P(('leaf', 'sub')), may hold values from -1 to 1023, as said below
- top_list: int32 [32, 6], P('leaf'), may hold values from -1 to 31, as said below
- inv_scale: float32 [8], replicated, may hold values from 0.15 to 0.5
- amplitude: float32 [1], replicated, may hold values from 0.03 to 0.1
- noise_var: float32 [1], replicated, may hold values from 0.2 to 1
Outputs:
- first_product: bfloat16 [8192, 32, 128], P(('leaf', 'sub'))
- second_product: bfloat16 [8192, 32, 128], P(('leaf', 'sub'))
Inputs may be any that keep to these rules, and one draw needn't show every extreme that they name: `near_list`: entry 0 of row i is i; the other entries of a row are distinct leaves j != i with |j - i| <= 64, or -1. `mid_list`: the entries of a row m are distinct middle clusters j != m with |j - m| <= 8, or -1. `top_list`: the entries of a row t are distinct top clusters other than t, or -1.
All inputs are finite; a program needn't handle non-finite values.
Results may differ from a plain program's by a relative error of at most 0.0042.
Values may be sent and summed in bfloat16 or wider, within the bound.
A program may use at most 128 MiB of HBM per device.

v0:
```python
import jax
import jax.numpy as jnp
from jax import lax
from jax.sharding import PartitionSpec as P

MATVECS = 2


def padded(block, sides, width):
    for axis, dim in sides:
        count = lax.axis_size(axis)
        forward = [(i, i + 1) for i in range(count - 1)]
        backward = [(target, source) for source, target in forward]
        low = lax.ppermute(
            lax.slice_in_dim(block, block.shape[dim] - width, None, axis=dim), axis, forward
        )
        high = lax.ppermute(lax.slice_in_dim(block, 0, width, axis=dim), axis, backward)
        block = jnp.concatenate([low, block, high], axis=dim)
    return block


def matern(left_side, right_side, inv_scale, amplitude):
    accumulated = None
    for feature in range(left_side.shape[-2]):
        difference = (
            left_side[..., feature, :, None] - right_side[..., feature, None, :]
        ) * inv_scale[feature]
        if accumulated is None:
            accumulated = difference * difference
        else:
            accumulated = accumulated + difference * difference
    scaled = jnp.sqrt(3.0 * accumulated)
    return amplitude * (1.0 + scaled) * jnp.exp(-scaled)


def on_device(
    points,
    probes,
    leaf_basis,
    mid_transfer,
    top_transfer,
    mid_skeleton,
    top_skeleton,
    near_list,
    mid_list,
    top_list,
    inv_scale,
    amplitude,
    noise_var,
):
    highest = lax.Precision.HIGHEST
    scale_amp = amplitude[0]
    leaf_dev = points.shape[0]
    mid_dev = mid_skeleton.shape[0]
    probe_count = probes.shape[1]
    rank = leaf_basis.shape[1]
    position = lax.axis_index("leaf") * lax.axis_size("sub") + lax.axis_index("sub")
    leaf_start = position * leaf_dev
    mid_start = position * mid_dev
    top_index = lax.axis_index("leaf")
    top_count = lax.axis_size("leaf")
    wide_points = padded(points, ((("leaf", "sub"), 0),), leaf_dev)
    near_present = near_list >= 0
    near_local = jnp.where(near_present, near_list - leaf_start + leaf_dev, 0)
    near_blocks = matern(points[:, None], wide_points[near_local], inv_scale, scale_amp)
    near_blocks = (near_blocks * near_present[:, :, None, None].astype(jnp.float32)).astype(
        jnp.bfloat16
    )
    wide_skeleton = padded(mid_skeleton, ((("leaf", "sub"), 0),), mid_dev)
    mid_present = mid_list >= 0
    mid_local_ids = jnp.where(mid_present, mid_list - mid_start + mid_dev, 0)
    mid_coupling = matern(mid_skeleton[:, None], wide_skeleton[mid_local_ids], inv_scale, scale_amp)
    mid_coupling = mid_coupling * mid_present[:, :, None, None].astype(jnp.float32)
    top_row = top_list[0]
    top_present = top_row >= 0
    top_clipped = jnp.where(top_present, top_row, 0)
    own_skeleton = lax.dynamic_index_in_dim(top_skeleton, top_index, 0, keepdims=True)
    top_coupling = matern(own_skeleton, top_skeleton[top_clipped], inv_scale, scale_amp)
    top_coupling = top_coupling * top_present[:, None, None].astype(jnp.float32)
    transfer_groups = mid_transfer.reshape(mid_dev, -1, rank, rank)
    slot_weights = (jnp.arange(top_count) == top_index).astype(jnp.float32)
    vector = probes
    results = []
    for matvec_turn in range(MATVECS):
        leaf_coef = jnp.einsum(
            "lpn,lrn->lpr", vector, leaf_basis, preferred_element_type=jnp.float32
        )
        leaf_groups = leaf_coef.reshape(mid_dev, -1, probe_count, rank)
        mid_coef = jnp.einsum("mcpr,mcrs->mps", leaf_groups, transfer_groups, precision=highest)
        wide_coef = padded(mid_coef, ((("leaf", "sub"), 0),), mid_dev)
        mid_local = jnp.einsum(
            "mkrs,mkps->mpr", mid_coupling, wide_coef[mid_local_ids], precision=highest
        )
        partial_top = jnp.einsum("mpr,mrs->ps", mid_coef, top_transfer, precision=highest)
        slots = slot_weights[:, None, None] * partial_top[None]
        all_top = lax.psum(slots, ("leaf", "sub"))
        top_local = jnp.einsum("krs,kps->pr", top_coupling, all_top[top_clipped], precision=highest)
        mid_total = mid_local + jnp.einsum(
            "ps,mrs->mpr", top_local, top_transfer, precision=highest
        )
        leaf_total = jnp.einsum("mps,mcrs->mcpr", mid_total, transfer_groups, precision=highest)
        leaf_total = leaf_total.reshape(leaf_dev, probe_count, rank).astype(jnp.bfloat16)
        far = jnp.einsum("lpr,lrn->lpn", leaf_total, leaf_basis, preferred_element_type=jnp.float32)
        wide_vector = padded(vector, ((("leaf", "sub"), 0),), leaf_dev)
        near = jnp.einsum(
            "iknm,ikpm->ipn",
            near_blocks,
            wide_vector[near_local],
            preferred_element_type=jnp.float32,
        )
        vector = (noise_var[0] * vector.astype(jnp.float32) + near + far).astype(jnp.bfloat16)
        results.append(vector)
    return (results[0], results[1])


def solution(mesh):
    in_specs = (
        P(("leaf", "sub"), None, None),
        P(("leaf", "sub"), None, None),
        P(("leaf", "sub"), None, None),
        P(("leaf", "sub"), None, None),
        P(("leaf", "sub"), None, None),
        P(("leaf", "sub"), None, None),
        P(),
        P(("leaf", "sub"), None),
        P(("leaf", "sub"), None),
        P("leaf", None),
        P(),
        P(),
        P(),
    )
    out_specs = (P(("leaf", "sub"), None, None), P(("leaf", "sub"), None, None))
    return jax.shard_map(
        on_device, mesh=mesh, in_specs=in_specs, out_specs=out_specs, check_vma=False
    )
```

profile of v0, /device:TPU:1, one launch (start us, length us, event | category | flops | bytes accessed | tf_op | source)
XLA Modules:
  0.0 522.9 jit_solution(7574531809006721191)
XLA Ops:
  7.2 5.9 %collective-permute-start.1 = (bf16[64,32,128]{2,1,0:T(8,128)(2,1)}, bf16[64,32,128]{2,1,0:T(8,128)(2,1)}, u32[]{:S(2)}, u32[]{:S(2)}) collective-permute-start(bf16[64,32,128]{2,1,0:T(8,128)(2,1)} %param.14), channel_id=1, source_target_pairs={{1,0},{2,1},{3,2},{4,3},{5,4},{6,5},{7,6},{8,7},{9,8},{10,9},{11,1... | collective-permute-start | bytes 1572872 | tf_op jit(solution)/shard_map/ppermute | solution.py:17
  13.1 1.9 collective-permute-start
  15.1 4.9 collective-permute-start.7
  19.9 1.9 collective-permute-start.6
  21.9 4.9 collective-permute-start.3
  26.7 2.0 fusion.28
  44.4 3.4 collective-permute-start.4
  51.1 2.1 collective-permute-start.2
  54.7 127.5 %all-reduce.3.cloned.1.call-done = f32[32,32,64]{2,1,0:T(8,128)} async-done(((f32[32,32,64]{2,1,0:T(8,128)}), f32[32,32,64]{2,1,0:T(8,128)}) %all-reduce.3.cloned.1.call-update) | async-done | bytes 262160 | tf_op jit(solution)/shard_map/psum | solution.py:96
  184.0 6.4 %fusion.9 = f32[32,64,1]{1,0,2:T(8,128)S(1)} fusion(f32[6,32,64]{2,1,0:T(8,128)S(1)} %gather_fusion.4, f32[6]{0:T(128)} %fusion.12, f32[]{:T(128)} %bitcast.28, f32[6,64]{1,0:T(8,128)} %get-tuple-element.58, f32[64]{0:T(128)} %get-tuple-element.43, f32[]{:T(128)} %bitcast.25, f32[6,64]{1,0:T(8,128)} %get-tuple-element.59, f32[64]{0:T(128)} %get-tuple-element.44, ...), kind=kOutput, calls=%fused_computation.43 | convolution fusion | flops 10346496 | bytes 71740 | tf_op jit(solution)/shard_map/krs,kps->pr/dot_general | solution.py:97
  191.5 9.8 %fusion.5 = f32[8,32,64,1]{2,1,3,0:T(8,128)S(1)} fusion(f32[8,32,64]{2,1,0:T(8,128)S(1)} %convolution_bitcast_fusion.6, f32[8,6,32,64]{3,2,1,0:T(8,128)S(1)} %bitcast.216, f32[8,6]{1,0:T(8,128)S(1)} %copy-done.58, f32[]{:T(128)} %bitcast.28, f32[8,6,64]{2,1,0:T(8,128)S(1)} %copy-done.24, f32[8,64]{1,0:T(8,128)S(1)} %bitcast.253, f32[]{:T(128)} %bitcast.25, ...), kind=kOutput, calls=%fused_computation.26 | convolution fusion | flops 82788352 | bytes 639204 | tf_op jit(solution)/shard_map/mkrs,mkps->mpr/dot_general | solution.py:91
  201.3 6.6 %convolution_convert_fusion.1 = bf16[8,32,8,64]{3,1,2,0:T(8,128)(2,1)} fusion(f32[8,32,64,1]{2,1,3,0:T(8,128)S(1)} %fusion.5, f32[8,8,64,64]{3,2,1,0:T(8,128)S(1)} %bitcast.204), kind=kOutput, calls=%fused_computation.22 | convolution fusion | flops 100794368 | bytes 1376256 | tf_op jit(solution)/shard_map/mps,mcrs->mcpr/dot_general | solution.py:101
  208.9 2.7 gather_fusion.1
  211.7 9.1 %fusion.22 = (f32[64,8,1,128]{3,2,1,0:T(1,128)S(1)}, f32[64,8,1,128]{3,2,1,0:T(1,128)S(1)}, f32[64,8,1,128]{3,2,1,0:T(1,128)S(1)}, f32[64,8,1,128]{3,2,1,0:T(1,1...) fusion(f32[64,8,8,128]{3,2,1,0:T(8,128)} %bitcast.209), kind=kLoop, calls=%fused_computation.92 | loop fusion | bytes 4194304 | tf_op jit(solution)/shard_map/slice | solution.py:26
  221.0 63.7 %multiply_convert_fusion.6 = bf16[64,8,128,128]{3,2,1,0:T(8,128)(2,1)} fusion(f32[64,8]{1,0:T(8,128)S(1)} %copy-done.40, f32[]{:T(128)} %bitcast.28, f32[64,8,128]{2,1,0:T(8,128)S(1)} %bitcast.232, f32[64,128]{1,0:T(8,128)S(1)} %bitcast.238, f32[]{:T(128)} %bitcast.25, f32[64,8,128]{2,1,0:T(8,128)S(1)} %bitcast.220, f32[64,128]{1,0:T(8,128)S(1)} %bitcast.240, ...), kind=kLoop, calls=%fused_computation.9.clone.1.clone | loop fusion | flops 318767104 | bytes 19138596 | tf_op jit(solution)/shard_map/iknm,ikpm->ipn/dot_general | solution.py:105
  284.8 2.5 pad_maximum_fusion
  287.3 4.7 gather_fusion
  292.0 13.9 %fusion.1 = f32[64,32,128]{2,1,0:T(8,128)} fusion(bf16[64,8,32,128]{3,2,1,0:T(8,128)(2,1)} %bitcast.208, bf16[64,32,128]{2,1,0:T(8,128)(2,1)} %param.14, f32[]{:T(128)} %bitcast.201, bf16[64,8,128,128]{3,2,1,0:T(8,128)(2,1)} %multiply_convert_fusion.6), kind=kOutput, calls=%fused_computation.18 | convolution fusion | flops 537657344 | bytes 22544388 | tf_op jit(solution)/shard_map/iknm,ikpm->ipn/dot_general | solution.py:105
  305.8 2.6 fusion.2
  311.8 3.5 collective-permute-start.11
  318.2 67.8 %multiply_convert_fusion.5 = bf16[64,8,128,128]{3,2,1,0:T(8,128)(2,1)} fusion(f32[64,8]{1,0:T(8,128)} %copy.27, f32[]{:T(128)} %bitcast.28, f32[64,8,128]{2,1,0:T(8,128)} %bitcast.233, f32[64,128]{1,0:T(8,128)} %bitcast.237, f32[]{:T(128)} %bitcast.25, f32[64,8,128]{2,1,0:T(8,128)} %bitcast.221, f32[64,128]{1,0:T(8,128)} %bitcast.239, ...), kind=kLoop, calls=%fused_computation.9.clone.clone.1 | loop fusion | flops 318767104 | bytes 19138596 | tf_op jit(solution)/shard_map/iknm,ikpm->ipn/dot_general | solution.py:105
  386.0 4.9 collective-permute-start.9
  390.9 1.9 collective-permute-start.8
  394.6 2.5 gather_fusion.7
  397.1 69.3 %all-reduce.5.cloned.1.call-done = f32[32,32,64]{2,1,0:T(8,128)} async-done(((f32[32,32,64]{2,1,0:T(8,128)}), f32[32,32,64]{2,1,0:T(8,128)}) %all-reduce.5.cloned.1.call-update) | async-done | bytes 262160 | tf_op jit(solution)/shard_map/psum | solution.py:96
  468.2 6.5 %fusion.8 = f32[32,64,1]{1,0,2:T(8,128)S(1)} fusion(f32[6,32,64]{2,1,0:T(8,128)S(1)} %gather_fusion.8, f32[6]{0:T(128)} %fusion.12, f32[]{:T(128)} %bitcast.28, f32[6,64]{1,0:T(8,128)} %get-tuple-element.58, f32[64]{0:T(128)} %get-tuple-element.43, f32[]{:T(128)} %bitcast.25, f32[6,64]{1,0:T(8,128)} %get-tuple-element.59, f32[64]{0:T(128)} %get-tuple-element.44, ...), kind=kOutput, calls=%fused_computation.42 | convolution fusion | flops 10346496 | bytes 71740 | tf_op jit(solution)/shard_map/krs,kps->pr/dot_general | solution.py:97
  475.6 10.1 %fusion.7 = f32[8,32,64,1]{2,1,3,0:T(8,128)S(1)} fusion(f32[8,32,64]{2,1,0:T(8,128)S(1)} %convolution_bitcast_fusion.4, f32[8,6,32,64]{3,2,1,0:T(8,128)S(1)} %bitcast.215, f32[8,6]{1,0:T(8,128)S(1)} %copy-done.59, f32[]{:T(128)} %bitcast.28, f32[8,6,64]{2,1,0:T(8,128)S(1)} %copy-done.25, f32[8,64]{1,0:T(8,128)S(1)} %bitcast.254, f32[]{:T(128)} %bitcast.25, ...), kind=kOutput, calls=%fused_computation.28 | convolution fusion | flops 82788352 | bytes 639204 | tf_op jit(solution)/shard_map/mkrs,mkps->mpr/dot_general | solution.py:91
  485.7 6.6 %convolution_convert_fusion = bf16[8,32,8,64]{3,1,2,0:T(8,128)(2,1)} fusion(f32[8,32,64,1]{2,1,3,0:T(8,128)S(1)} %fusion.7, f32[8,8,64,64]{3,2,1,0:T(8,128)S(1)} %bitcast.206), kind=kOutput, calls=%fused_computation.21 | convolution fusion | flops 100794368 | bytes 1376256 | tf_op jit(solution)/shard_map/mps,mcrs->mcpr/dot_general | solution.py:101
  492.3 2.7 pad_maximum_fusion.1
  495.0 4.7 gather_fusion.6
  499.7 13.8 %fusion = f32[64,32,128]{2,1,0:T(8,128)} fusion(bf16[64,8,32,128]{3,2,1,0:T(8,128)(2,1)} %bitcast.207, bf16[64,32,128]{2,1,0:T(8,128)(2,1)} %fusion.2, f32[]{:T(128)} %bitcast.202, bf16[64,8,128,128]{3,2,1,0:T(8,128)(2,1)} %multiply_convert_fusion.5), kind=kOutput, calls=%fused_computation.15 | convolution fusion | flops 537657344 | bytes 22544388 | tf_op jit(solution)/shard_map/iknm,ikpm->ipn/dot_general | solution.py:105
  513.5 2.6 fusion.3
  (191 shorter events, 33.1 us)
Async XLA Ops:
  7.2 21.6 %copy-start = (f32[64,64,64]{2,1,0:T(8,128)S(1)}, f32[64,64,64]{2,1,0:T(8,128)}, u32[]{:S(2)}) copy-start(f32[64,64,64]{2,1,0:T(8,128)} %param.16) | copy-start | bytes 3145732
  7.2 175.1 %all-reduce.3.cloned.1.call-start = ((), (), s32[]{:S(2)}) async-start(), calls=%async_computation | async-start | bytes 1048576 | tf_op jit(solution)/shard_map/psum | solution.py:96
  7.2 277.5 %collective-permute-start.1 = (bf16[64,32,128]{2,1,0:T(8,128)(2,1)}, bf16[64,32,128]{2,1,0:T(8,128)(2,1)}, u32[]{:S(2)}, u32[]{:S(2)}) collective-permute-start(bf16[64,32,128]{2,1,0:T(8,128)(2,1)} %param.14), channel_id=1, source_target_pairs={{1,0},{2,1},{3,2},{4,3},{5,4},{6,5},{7,6},{8,7},{9,8},{10,9},{11,1... | collective-permute-start | bytes 1572872 | tf_op jit(solution)/shard_map/ppermute | solution.py:17
  13.1 271.6 %collective-permute-start = (bf16[64,32,128]{2,1,0:T(8,128)(2,1)}, bf16[64,32,128]{2,1,0:T(8,128)(2,1)}, u32[]{:S(2)}, u32[]{:S(2)}) collective-permute-start(bf16[64,32,128]{2,1,0:T(8,128)(2,1)} %param.14), channel_id=1, source_target_pairs={{0,1},{1,2},{2,3},{3,4},{4,5},{5,6},{6,7},{7,8},{8,9},{9,10},{10,1... | collective-permute-start | bytes 1572872 | tf_op jit(solution)/shard_map/ppermute | solution.py:14
  15.1 27.4 %collective-permute-start.7 = (f32[8,8,64]{2,1,0:T(8,128)}, f32[8,8,64]{2,1,0:T(8,128)S(1)}, u32[]{:S(2)}, u32[]{:S(2)}) collective-permute-start(f32[8,8,64]{2,1,0:T(8,128)} %param.18), channel_id=1, source_target_pairs={{1,0},{2,1},{3,2},{4,3},{5,4},{6,5},{7,6},{8,7},{9,8},{10,9},{11,1... | collective-permute-start | bytes 49160 | tf_op jit(solution)/shard_map/ppermute | solution.py:17
  19.9 24.5 %collective-permute-start.6 = (f32[8,8,64]{2,1,0:T(8,128)}, f32[8,8,64]{2,1,0:T(8,128)S(1)}, u32[]{:S(2)}, u32[]{:S(2)}) collective-permute-start(f32[8,8,64]{2,1,0:T(8,128)} %param.18), channel_id=1, source_target_pairs={{0,1},{1,2},{2,3},{3,4},{4,5},{5,6},{6,7},{7,8},{8,9},{9,10},{10,1... | collective-permute-start | bytes 49160 | tf_op jit(solution)/shard_map/ppermute | solution.py:14
  21.9 186.0 %collective-permute-start.3 = (f32[64,8,128]{2,1,0:T(8,128)}, f32[64,8,128]{2,1,0:T(8,128)}, u32[]{:S(2)}, u32[]{:S(2)}) collective-permute-start(f32[64,8,128]{2,1,0:T(8,128)} %param.13), channel_id=1, source_target_pairs={{1,0},{2,1},{3,2},{4,3},{5,4},{6,5},{7,6},{8,7},{9,8},{10,9},{11,1... | collective-permute-start | bytes 786440 | tf_op jit(solution)/shard_map/ppermute | solution.py:17
  31.5 434.9 %all-reduce.5.cloned.1.call-start = ((), (), s32[]{:S(2)}) async-start(), calls=%async_computation.1 | async-start | bytes 1048576 | tf_op jit(solution)/shard_map/psum | solution.py:96
  42.5 8.6 %collective-permute-start.5 = (f32[8,32,64]{2,1,0:T(8,128)S(1)}, f32[8,32,64]{2,1,0:T(8,128)S(1)}, u32[]{:S(2)}, u32[]{:S(2)}) collective-permute-start(f32[8,32,64]{2,1,0:T(8,128)S(1)} %convolution_bitcast_fusion.7), channel_id=1, source_target_pairs={{1,0},{2,1},{3,2},{4,3},{5,4},{6,5},{7,6},{8,7},{9,8},{10,9},{11,1... | collective-permute-start | bytes 196616 | tf_op jit(solution)/shard_map/ppermute | solution.py:17
  44.4 8.8 %collective-permute-start.4 = (f32[8,32,64]{2,1,0:T(8,128)S(1)}, f32[8,32,64]{2,1,0:T(8,128)S(1)}, u32[]{:S(2)}, u32[]{:S(2)}) collective-permute-start(f32[8,32,64]{2,1,0:T(8,128)S(1)} %convolution_bitcast_fusion.7), channel_id=1, source_target_pairs={{0,1},{1,2},{2,3},{3,4},{4,5},{5,6},{6,7},{7,8},{8,9},{9,10},{10,1... | collective-permute-start | bytes 196616 | tf_op jit(solution)/shard_map/ppermute | solution.py:14
  51.1 156.8 %collective-permute-start.2 = (f32[64,8,128]{2,1,0:T(8,128)S(1)}, f32[64,8,128]{2,1,0:T(8,128)}, u32[]{:S(2)}, u32[]{:S(2)}) collective-permute-start(f32[64,8,128]{2,1,0:T(8,128)S(1)} %copy-done.4), channel_id=1, source_target_pairs={{0,1},{1,2},{2,3},{3,4},{4,5},{5,6},{6,7},{7,8},{8,9},{9,10},{10,1... | collective-permute-start | bytes 786440 | tf_op jit(solution)/shard_map/ppermute | solution.py:14
  53.2 138.1 %copy-start.24 = (f32[8,6,64]{2,1,0:T(8,128)S(1)}, f32[8,6,64]{2,1,0:T(8,128)}, u32[]{:S(2)}) copy-start(f32[8,6,64]{2,1,0:T(8,128)} %get-tuple-element.66) | copy-start | bytes 36868
  54.7 136.5 %copy-start.6 = (f32[48,32,64]{2,1,0:T(8,128)S(1)}, f32[48,32,64]{2,1,0:T(8,128)}, u32[]{:S(2)}) copy-start(f32[48,32,64]{2,1,0:T(8,128)} %gather_fusion.2) | copy-start | bytes 1179652
  211.7 9.3 %copy-start.20 = (f32[64,1,1,128]{3,2,0,1:T(1,128)S(1)}, f32[64,1,1,128]{3,2,0,1:T(1,128)}, u32[]{:S(2)}) copy-start(f32[64,1,1,128]{3,2,0,1:T(1,128)} %get-tuple-element.14) | copy-start | bytes 98308
  211.7 9.3 %copy-start.21 = (f32[64,1,1,128]{3,2,0,1:T(1,128)S(1)}, f32[64,1,1,128]{3,2,0,1:T(1,128)}, u32[]{:S(2)}) copy-start(f32[64,1,1,128]{3,2,0,1:T(1,128)} %get-tuple-element.15) | copy-start | bytes 98308
  211.7 9.3 %copy-start.22 = (f32[64,1,1,128]{3,2,0,1:T(1,128)S(1)}, f32[64,1,1,128]{3,2,0,1:T(1,128)}, u32[]{:S(2)}) copy-start(f32[64,1,1,128]{3,2,0,1:T(1,128)} %get-tuple-element.16) | copy-start | bytes 98308
  220.8 63.9 %copy-start.7 = (f32[64,8,1,128]{3,2,1,0:T(1,128)}, f32[64,8,1,128]{3,2,1,0:T(1,128)S(1)}, u32[]{:S(2)}) copy-start(f32[64,8,1,128]{3,2,1,0:T(1,128)S(1)} %get-tuple-element.2) | copy-start | bytes 786436
  220.8 63.9 %copy-start.8 = (f32[64,8,1,128]{3,2,1,0:T(1,128)}, f32[64,8,1,128]{3,2,1,0:T(1,128)S(1)}, u32[]{:S(2)}) copy-start(f32[64,8,1,128]{3,2,1,0:T(1,128)S(1)} %get-tuple-element.3) | copy-start | bytes 786436
  220.8 63.9 %copy-start.9 = (f32[64,8,1,128]{3,2,1,0:T(1,128)}, f32[64,8,1,128]{3,2,1,0:T(1,128)S(1)}, u32[]{:S(2)}) copy-start(f32[64,8,1,128]{3,2,1,0:T(1,128)S(1)} %get-tuple-element.4) | copy-start | bytes 786436
  220.8 63.9 %copy-start.10 = (f32[64,8,1,128]{3,2,1,0:T(1,128)}, f32[64,8,1,128]{3,2,1,0:T(1,128)S(1)}, u32[]{:S(2)}) copy-start(f32[64,8,1,128]{3,2,1,0:T(1,128)S(1)} %get-tuple-element.5) | copy-start | bytes 786436
  220.8 63.9 %copy-start.11 = (f32[64,8,1,128]{3,2,1,0:T(1,128)}, f32[64,8,1,128]{3,2,1,0:T(1,128)S(1)}, u32[]{:S(2)}) copy-start(f32[64,8,1,128]{3,2,1,0:T(1,128)S(1)} %get-tuple-element.6) | copy-start | bytes 786436
  220.8 63.9 %copy-start.12 = (f32[64,8,1,128]{3,2,1,0:T(1,128)}, f32[64,8,1,128]{3,2,1,0:T(1,128)S(1)}, u32[]{:S(2)}) copy-start(f32[64,8,1,128]{3,2,1,0:T(1,128)S(1)} %get-tuple-element.7) | copy-start | bytes 786436
  220.8 63.9 %copy-start.13 = (f32[64,8,1,128]{3,2,1,0:T(1,128)}, f32[64,8,1,128]{3,2,1,0:T(1,128)S(1)}, u32[]{:S(2)}) copy-start(f32[64,8,1,128]{3,2,1,0:T(1,128)S(1)} %get-tuple-element.8) | copy-start | bytes 786436
  220.9 63.9 %copy-start.14 = (f32[64,8,1,128]{3,2,1,0:T(1,128)}, f32[64,8,1,128]{3,2,1,0:T(1,128)S(1)}, u32[]{:S(2)}) copy-start(f32[64,8,1,128]{3,2,1,0:T(1,128)S(1)} %get-tuple-element.9) | copy-start | bytes 786436
  221.0 63.8 %copy-start.2 = (bf16[64,32,128]{2,1,0:T(8,128)(2,1)S(1)}, bf16[64,32,128]{2,1,0:T(8,128)(2,1)}, u32[]{:S(2)}) copy-start(bf16[64,32,128]{2,1,0:T(8,128)(2,1)} %param.14) | copy-start | bytes 1572868
  291.9 13.9 %copy-start.1 = (bf16[64,64,128]{2,1,0:T(8,128)(2,1)S(1)}, bf16[64,64,128]{2,1,0:T(8,128)(2,1)}, u32[]{:S(2)}) copy-start(bf16[64,64,128]{2,1,0:T(8,128)(2,1)} %param.15) | copy-start | bytes 3145732
  311.8 81.0 %collective-permute-start.11 = (f32[8,32,64]{2,1,0:T(8,128)S(1)}, f32[8,32,64]{2,1,0:T(8,128)}, u32[]{:S(2)}, u32[]{:S(2)}) collective-permute-start(f32[8,32,64]{2,1,0:T(8,128)S(1)} %convolution_bitcast_fusion.5), channel_id=1, source_target_pairs={{1,0},{2,1},{3,2},{4,3},{5,4},{6,5},{7,6},{8,7},{9,8},{10,9},{11,1... | collective-permute-start | bytes 196616 | tf_op jit(solution)/shard_map/ppermute | solution.py:17
  315.4 77.5 %collective-permute-start.10 = (f32[8,32,64]{2,1,0:T(8,128)S(1)}, f32[8,32,64]{2,1,0:T(8,128)}, u32[]{:S(2)}, u32[]{:S(2)}) collective-permute-start(f32[8,32,64]{2,1,0:T(8,128)S(1)} %convolution_bitcast_fusion.5), channel_id=1, source_target_pairs={{0,1},{1,2},{2,3},{3,4},{4,5},{5,6},{6,7},{7,8},{8,9},{9,10},{10,1... | collective-permute-start | bytes 196616 | tf_op jit(solution)/shard_map/ppermute | solution.py:14
  386.0 106.3 %collective-permute-start.9 = (bf16[64,32,128]{2,1,0:T(8,128)(2,1)}, bf16[64,32,128]{2,1,0:T(8,128)(2,1)}, u32[]{:S(2)}, u32[]{:S(2)}) collective-permute-start(bf16[64,32,128]{2,1,0:T(8,128)(2,1)} %fusion.2), channel_id=1, source_target_pairs={{1,0},{2,1},{3,2},{4,3},{5,4},{6,5},{7,6},{8,7},{9,8},{10,9},{11,1... | collective-permute-start | bytes 1572872 | tf_op jit(solution)/shard_map/ppermute | solution.py:17
  390.9 101.4 %collective-permute-start.8 = (bf16[64,32,128]{2,1,0:T(8,128)(2,1)}, bf16[64,32,128]{2,1,0:T(8,128)(2,1)}, u32[]{:S(2)}, u32[]{:S(2)}) collective-permute-start(bf16[64,32,128]{2,1,0:T(8,128)(2,1)} %fusion.2), channel_id=1, source_target_pairs={{0,1},{1,2},{2,3},{3,4},{4,5},{5,6},{6,7},{7,8},{8,9},{9,10},{10,1... | collective-permute-start | bytes 1572872 | tf_op jit(solution)/shard_map/ppermute | solution.py:14
  394.6 80.9 %copy-start.25 = (f32[8,6,64]{2,1,0:T(8,128)S(1)}, f32[8,6,64]{2,1,0:T(8,128)}, u32[]{:S(2)}) copy-start(f32[8,6,64]{2,1,0:T(8,128)} %get-tuple-element.66) | copy-start | bytes 36868
  397.1 78.4 %copy-start.45 = (f32[8,1,1,64]{3,2,0,1:T(1,128)S(1)}, f32[8,1,1,64]{3,2,0,1:T(1,128)}, u32[]{:S(2)}) copy-start(f32[8,1,1,64]{3,2,0,1:T(1,128)} %get-tuple-element.27) | copy-start | bytes 6148
  (45 other events, 320.8 us)
Sparse Core Ops, SparseCore 0:
  31.6 150.6 all-reduce.2
  318.4 147.9 all-reduce.4
where the time goes:
time: 524 us; the launch traced here: 523 us
  waiting for transfers between devices  197 us (38%)
  other arithmetic  143 us (27%)
  matrix products  87.6 us (17%)
  local copies, waits for them, and re-layouts  40.1 us (8%)
  starting transfers between devices  39.2 us (7%)
  between operations  16.5 us (3%)
    psum x2, waiting for transfers between devices, on_device(): all_top = lax.psum(slots, ('leaf', 'sub'))  197 us
    dot_general x2, other arithmetic, on_device(): jnp.einsum('iknm,ikpm->ipn', near_blocks, wide_vector[near_local], prefer...  131 us
    dot_general x2, matrix products, on_device(): jnp.einsum('iknm,ikpm->ipn', near_blocks, wide_vector[near_local], prefer...  27.7 us
    ppermute x6, starting transfers between devices, padded(): lax.ppermute(lax.slice_in_dim(block, 0, width, axis=dim), axis, backward)  25.9 us
    dot_general x2, matrix products, on_device(): jnp.einsum('mkrs,mkps->mpr', mid_coupling, wide_coef[mid_local_ids], prec...  19.9 us
    ppermute x6, starting transfers between devices, padded(): lax.ppermute(lax.slice_in_dim(block, block.shape[dim] - width, None, axis...  13.1 us
    dot_general x2, matrix products, on_device(): jnp.einsum('mps,mcrs->mcpr', mid_total, transfer_groups, precision=highest)  13.1 us
    dot_general x2, matrix products, on_device(): jnp.einsum('krs,kps->pr', top_coupling, all_top[top_clipped], precision=h...  12.9 us
  transfers between devices with their start and end apart: 14, of which 2 were waited for; matrix products, arithmetic and copies ran while one was open for 42% of the time, Pallas kernels for 0%

commit v1 on v0

v1 whole, which is shorter than its diff:
```python
import functools
import math

import jax
import jax.numpy as jnp
from jax import lax
from jax.experimental import pallas as pl
from jax.experimental.pallas import tpu as pltpu
from jax.sharding import PartitionSpec as P

MESH = pl.DeviceIdType.MESH
F32 = jnp.float32
BF16 = jnp.bfloat16
LEAFS = 64
MIDS = 8
GROUP = 8
NEAR = 8
MID_NEAR = 6
TOP_NEAR = 6
TOPS = 32
SUBS = 4
R = 64
PROBES = 32
POINTS = 128
CHUNKS = 4
LOG2E = math.log2(math.e)
LN2 = math.log(2.0)
TINY = 1e-30


def nn(a, b):
    return lax.dot_general(a, b, (((1,), (0,)), ((), ())), preferred_element_type=F32)


def nt(a, b):
    return lax.dot_general(a, b, (((1,), (1,)), ((), ())), preferred_element_type=F32)


def split(a):
    high = a.astype(BF16)
    return high, (a - high.astype(F32)).astype(BF16)


def stacked(a):
    return jnp.concatenate(split(a), axis=0)


def wide_product(both, high, low, op):
    rows = both.shape[0] // 2
    result = op(both, high)
    return result[:rows] + result[rows:] + op(both[:rows], low)


def pack(a):
    half = a.shape[0] // 2
    return jnp.concatenate([a[:half], a[half:]], axis=1)


def unpack(a):
    half = a.shape[1] // 2
    return jnp.concatenate([a[:, :half], a[:, half:]], axis=0)


def three(x):
    high = x.astype(BF16).astype(F32)
    rest = x - high
    mid = rest.astype(BF16).astype(F32)
    low = (rest - mid).astype(BF16).astype(F32)
    return high, mid, low


def features(x, left, right):
    width = x.shape[1]
    high, mid, low = three(x)
    norms = jnp.broadcast_to(jnp.sum(x * x, axis=0, keepdims=True), (8, width))
    norm_high, norm_mid, norm_low = three(norms)
    row = lax.broadcasted_iota(jnp.int32, (8, width), 0)
    one = jnp.ones((8, width), F32)
    zero = jnp.zeros((8, width), F32)
    result = []
    if left:
        extra = jnp.where(row < 3, one, zero)
        for place, part in ((3, norm_high), (4, norm_mid), (5, norm_low)):
            extra = jnp.where(row == place, part, extra)
        result.append(jnp.concatenate([high, high, high, mid, mid, low, extra, zero], axis=0))
    if right:
        extra = jnp.where((row >= 3) & (row < 6), one, zero)
        for place, part in ((0, norm_high), (1, norm_mid), (2, norm_low)):
            extra = jnp.where(row == place, part, extra)
        h, m, l = -2.0 * high, -2.0 * mid, -2.0 * low
        result.append(jnp.concatenate([h, m, l, h, m, h, extra, zero], axis=0))
    return result


def matern(squared, amplitude):
    squared = jnp.maximum(squared, TINY)
    u = squared * lax.rsqrt(squared)
    return (amplitude + (amplitude * LN2) * u) * jnp.exp2(-u)


def device_at(position):
    count = TOPS * SUBS
    position = lax.rem(position + count, count)
    return (lax.div(position, SUBS), lax.rem(position, SUBS))


def kernel(
    points_ref,
    probes_ref,
    basis_ref,
    transfer_ref,
    top_transfer_ref,
    mid_skeleton_ref,
    top_skeleton_ref,
    near_list,
    mid_list,
    top_list,
    inv_scale,
    amplitude,
    noise_var,
    first_ref,
    second_ref,
    points_v,
    vector_0,
    vector_1,
    result_v,
    basis,
    transfer_v,
    transfer_h,
    transfer_l,
    top_v,
    top_h,
    top_l,
    skeleton,
    left_v,
    right_v,
    blocks,
    mid_left,
    coupling_h,
    coupling_l,
    top_coupling_h,
    top_coupling_l,
    mids_0,
    mids_1,
    mid_both,
    leaf_total,
    sums_0,
    sums_1,
    tops_0,
    tops_1,
    local_sem,
    out_sem,
    bulk_send,
    bulk_recv,
    side_send,
    side_recv,
    sub_send,
    sub_recv,
    near_send,
    near_recv,
    far_send,
    far_recv,
):
    leaf = lax.axis_index("leaf")
    sub = lax.axis_index("sub")
    position = leaf * SUBS + sub
    plane = lax.div(leaf, 8)
    place = lax.rem(leaf, 8)
    before = device_at(position - 1)
    after = device_at(position + 1)
    sub_ids = [(leaf, lax.rem(sub + k, SUBS)) for k in range(1, SUBS)]
    near_ids = [(plane * 8 + lax.rem(place + k, 8), sub) for k in range(1, 8)]
    far_ids = [(lax.rem(leaf + 8 * k, TOPS), sub) for k in range(1, 4)]

    barrier = pltpu.get_barrier_semaphore()
    partners = [before, after, *sub_ids, *near_ids, *far_ids]
    for partner in partners:
        pl.semaphore_signal(barrier, inc=1, device_id=partner, device_id_type=MESH)

    own = pl.ds(LEAFS, LEAFS)
    loads = [
        pltpu.make_async_copy(source, target, local_sem.at[k])
        for k, (source, target) in enumerate(
            (
                (probes_ref, vector_0.at[own]),
                (basis_ref, basis),
                (transfer_ref, transfer_v),
                (top_transfer_ref, top_v),
                (points_ref, points_v.at[own]),
                (mid_skeleton_ref, skeleton.at[pl.ds(MIDS, MIDS)]),
            )
        )
    ]
    for load in loads:
        load.start()
    pl.semaphore_wait(barrier, len(partners))

    def remote(source, target, send, recv, device):
        return pltpu.make_async_remote_copy(
            src_ref=source,
            dst_ref=target,
            send_sem=send,
            recv_sem=recv,
            device_id=device,
            device_id_type=MESH,
        )

    def halo(source, start, target, first, count, total, send, recv):
        rows = pl.ds(start + first, count)
        return [
            remote(source.at[rows], target.at[pl.ds(first, count)], send.at[0], recv.at[0], after),
            remote(
                source.at[rows],
                target.at[pl.ds(2 * total + first, count)],
                send.at[1],
                recv.at[1],
                before,
            ),
        ]

    per_chunk = LEAFS // CHUNKS
    points_halo = halo(
        points_ref, 0, points_v, 0, LEAFS, LEAFS, side_send.at[0], side_recv.at[0]
    )
    skeleton_halo = halo(
        mid_skeleton_ref, 0, skeleton, 0, MIDS, MIDS, side_send.at[1], side_recv.at[1]
    )
    probes_halo = [
        halo(
            probes_ref,
            0,
            vector_0,
            k * per_chunk,
            per_chunk,
            LEAFS,
            bulk_send.at[0, k],
            bulk_recv.at[0, k],
        )
        for k in range(CHUNKS)
    ]
    for copy in [*points_halo, *skeleton_halo, *probes_halo[0], *probes_halo[1]]:
        copy.start()

    row = lax.broadcasted_iota(jnp.int32, (8, POINTS), 0)
    scales = jnp.zeros((8, POINTS), F32)
    for feature in range(8):
        scales = jnp.where(row == feature, inv_scale[feature] * (math.sqrt(3.0) * LOG2E), scales)

    amp = amplitude[0]
    noise = noise_var[0]

    for load in loads[:4]:
        load.wait()

    def split_transfer(c, carry):
        transfer_h[c], transfer_l[c] = split(transfer_v[c])
        return carry

    lax.fori_loop(0, LEAFS, split_transfer, 0)
    for m in range(MIDS):
        top_h[m], top_l[m] = split(top_v[m])

    def upward(vector, mids, sums):
        def step(m, partial):
            total = jnp.zeros((PROBES, R), F32)
            for c in range(GROUP):
                leaf_id = m * GROUP + c
                coef = nt(vector[LEAFS + leaf_id], basis[leaf_id])
                total += wide_product(stacked(coef), transfer_h[leaf_id], transfer_l[leaf_id], nn)
            mids[MIDS + m] = pack(total)
            both = stacked(total)
            mid_both[MIDS + m] = both
            return partial + wide_product(both, top_h[m], top_l[m], nn)

        partial = lax.fori_loop(0, MIDS, step, jnp.zeros((PROBES, R), F32))
        sums[sub] = pack(partial)

    def small_copies(turn, mids, sums, tops):
        sides = halo(mids, MIDS, mids, 0, MIDS, MIDS, side_send.at[2 + turn], side_recv.at[2 + turn])
        in_sub = [
            remote(sums.at[sub], sums.at[sub], sub_send.at[turn, k], sub_recv.at[turn, k], device)
            for k, device in enumerate(sub_ids)
        ]
        in_plane = [
            remote(
                tops.at[leaf], tops.at[leaf], near_send.at[turn, k], near_recv.at[turn, k], device
            )
            for k, device in enumerate(near_ids)
        ]
        rows = pl.ds(plane * 8, 8)
        over_planes = [
            remote(
                tops.at[rows], tops.at[rows], far_send.at[turn, k], far_recv.at[turn, k], device
            )
            for k, device in enumerate(far_ids)
        ]
        return sides, in_sub, in_plane, over_planes

    def begin(copies):
        for copy in copies:
            copy.start()

    def finish(copies):
        for copy in copies:
            copy.wait()

    def sum_tops(sums, tops):
        total = sums[0]
        for k in range(1, SUBS):
            total += sums[k]
        tops[leaf] = total

    def mid_target(m, e):
        listed = mid_list[m, e]
        target = listed - position * MIDS + MIDS
        return listed, jnp.clip(target, 0, 3 * MIDS - 1)

    def downward(mids, tops):
        def take(m, carry):
            mid_both[m] = stacked(unpack(mids[m]))
            return carry

        lax.fori_loop(0, MIDS, take, 0)
        lax.fori_loop(2 * MIDS, 3 * MIDS, take, 0)
        top_local = jnp.zeros((PROBES, R), F32)
        for e in range(TOP_NEAR):
            target = jnp.clip(top_list[0, e], 0, TOPS - 1)
            top_local += wide_product(
                stacked(unpack(tops[target])), top_coupling_h[e], top_coupling_l[e], nn
            )
        top_both = stacked(top_local)

        def step(m, carry):
            total = wide_product(top_both, top_h[m], top_l[m], nt)
            for e in range(MID_NEAR):
                _, target = mid_target(m, e)
                total += wide_product(mid_both[target], coupling_h[m, e], coupling_l[m, e], nn)
            both = stacked(total)
            for c in range(GROUP):
                leaf_id = m * GROUP + c
                leaf_total[leaf_id] = wide_product(
                    both, transfer_h[leaf_id], transfer_l[leaf_id], nt
                ).astype(BF16)
            return carry

        lax.fori_loop(0, MIDS, step, 0)

    def near_target(i, e):
        listed = near_list[i, e]
        target = listed - position * LEAFS + LEAFS
        return listed, jnp.clip(target, 0, 3 * LEAFS - 1)

    def products(vector, result, offset, first, count):
        def step(i, carry):
            parts = []
            for e in range(NEAR):
                _, target = near_target(i, e)
                parts.append(vector[target])
            total = nn(jnp.concatenate(parts, axis=1), blocks[i])
            total += nn(leaf_total[i], basis[i])
            total += noise * vector[LEAFS + i].astype(F32)
            result[offset + i] = total.astype(BF16)
            return carry

        lax.fori_loop(first, first + count, step, 0, unroll=2)

    sides, in_sub, in_plane, over_planes = small_copies(0, mids_0, sums_0, tops_0)
    upward(vector_0, mids_0, sums_0)
    begin(in_sub)
    begin(sides)
    for k in range(2, CHUNKS):
        begin(probes_halo[k])

    loads[4].wait()

    def own_features(i, carry):
        left, right = features(points_v[LEAFS + i] * scales, True, True)
        left_v[LEAFS + i] = left.T.astype(BF16)
        right_v[i] = right.astype(BF16)
        return carry

    lax.fori_loop(0, LEAFS, own_features, 0, unroll=2)

    small_scales = scales[:, :R]
    (top_right,) = features(top_skeleton_ref[leaf] * small_scales, False, True)
    for e in range(TOP_NEAR):
        target = top_list[0, e]
        (top_left,) = features(
            top_skeleton_ref[jnp.clip(target, 0, TOPS - 1)] * small_scales, True, False
        )
        squared = nn(top_left.T.astype(BF16), top_right.astype(BF16))
        value = matern(squared, jnp.where(target >= 0, amp, 0.0))
        top_coupling_h[e], top_coupling_l[e] = split(value)

    finish(in_sub)
    sum_tops(sums_0, tops_0)
    begin(in_plane)

    finish(points_halo)

    def halo_features(i, carry):
        (left,) = features(points_v[i] * scales, True, False)
        left_v[i] = left.T.astype(BF16)
        return carry

    lax.fori_loop(0, LEAFS, halo_features, 0, unroll=2)
    lax.fori_loop(2 * LEAFS, 3 * LEAFS, halo_features, 0, unroll=2)
    finish(in_plane)
    begin(over_planes)

    def near_blocks(i, carry):
        right = right_v[i]
        for e in range(NEAR):
            listed, target = near_target(i, e)
            value = matern(nn(left_v[target], right), jnp.where(listed >= 0, amp, 0.0))
            blocks[i, pl.ds(e * POINTS, POINTS)] = value.astype(BF16)
        return carry

    lax.fori_loop(0, LEAFS, near_blocks, 0)

    loads[5].wait()
    finish(skeleton_halo)

    def mid_features(m, carry):
        (left,) = features(skeleton[m] * small_scales, True, False)
        mid_left[m] = left.T.astype(BF16)
        return carry

    lax.fori_loop(0, 3 * MIDS, mid_features, 0)

    def mid_couplings(m, carry):
        (right,) = features(skeleton[MIDS + m] * small_scales, False, True)
        right = right.astype(BF16)
        for e in range(MID_NEAR):
            listed, target = mid_target(m, e)
            value = matern(nn(mid_left[target], right), jnp.where(listed >= 0, amp, 0.0))
            coupling_h[m, e], coupling_l[m, e] = split(value)
        return carry

    lax.fori_loop(0, MIDS, mid_couplings, 0)

    finish(over_planes)
    finish(sides)
    downward(mids_0, tops_0)
    for chunk in probes_halo:
        finish(chunk)

    first_halo = [
        halo(
            vector_1,
            LEAFS,
            vector_1,
            k * per_chunk,
            per_chunk,
            LEAFS,
            bulk_send.at[1, k],
            bulk_recv.at[1, k],
        )
        for k in range(CHUNKS)
    ]
    sides, in_sub, in_plane, over_planes = small_copies(1, mids_1, sums_1, tops_1)
    for k in range(CHUNKS):
        products(vector_0, vector_1, LEAFS, k * per_chunk, per_chunk)
        if k < CHUNKS // 2:
            begin(first_halo[k])
    upward(vector_1, mids_1, sums_1)
    begin(in_sub)
    begin(sides)
    for k in range(CHUNKS // 2, CHUNKS):
        begin(first_halo[k])
    first_out = pltpu.make_async_copy(vector_1.at[own], first_ref, out_sem.at[CHUNKS])
    first_out.start()

    finish(in_sub)
    sum_tops(sums_1, tops_1)
    begin(in_plane)
    finish(in_plane)
    begin(over_planes)
    finish(over_planes)
    finish(sides)
    downward(mids_1, tops_1)
    for chunk in first_halo:
        finish(chunk)
    outs = []
    for k in range(CHUNKS):
        rows = pl.ds(k * per_chunk, per_chunk)
        products(vector_1, result_v, 0, k * per_chunk, per_chunk)
        out = pltpu.make_async_copy(result_v.at[rows], second_ref.at[rows], out_sem.at[k])
        out.start()
        outs.append(out)
    for out in outs:
        out.wait()
    first_out.wait()


def on_device(*arguments):
    hbm = pl.BlockSpec(memory_space=pl.ANY)
    smem = pl.BlockSpec(memory_space=pltpu.SMEM)
    vmem = pl.BlockSpec(memory_space=pltpu.VMEM)
    dma = pltpu.SemaphoreType.DMA
    wide = (3 * LEAFS, PROBES, POINTS)
    result = jax.ShapeDtypeStruct((LEAFS, PROBES, POINTS), BF16)
    return pl.pallas_call(
        kernel,
        out_shape=(result, result),
        in_specs=[hbm] * 6 + [vmem] + [smem] * 6,
        out_specs=(hbm, hbm),
        scratch_shapes=[
            pltpu.VMEM((3 * LEAFS, 8, POINTS), F32),
            pltpu.VMEM(wide, BF16),
            pltpu.VMEM(wide, BF16),
            pltpu.VMEM((LEAFS, PROBES, POINTS), BF16),
            pltpu.VMEM((LEAFS, R, POINTS), BF16),
            pltpu.VMEM((LEAFS, R, R), F32),
            pltpu.VMEM((LEAFS, R, R), BF16),
            pltpu.VMEM((LEAFS, R, R), BF16),
            pltpu.VMEM((MIDS, R, R), F32),
            pltpu.VMEM((MIDS, R, R), BF16),
            pltpu.VMEM((MIDS, R, R), BF16),
            pltpu.VMEM((3 * MIDS, 8, R), F32),
            pltpu.VMEM((3 * LEAFS, POINTS, R), BF16),
            pltpu.VMEM((LEAFS, R, POINTS), BF16),
            pltpu.VMEM((LEAFS, NEAR * POINTS, POINTS), BF16),
            pltpu.VMEM((3 * MIDS, R, R), BF16),
            pltpu.VMEM((MIDS, MID_NEAR, R, R), BF16),
            pltpu.VMEM((MIDS, MID_NEAR, R, R), BF16),
            pltpu.VMEM((TOP_NEAR, R, R), BF16),
            pltpu.VMEM((TOP_NEAR, R, R), BF16),
            pltpu.VMEM((3 * MIDS, PROBES // 2, 2 * R), F32),
            pltpu.VMEM((3 * MIDS, PROBES // 2, 2 * R), F32),
            pltpu.VMEM((3 * MIDS, 2 * PROBES, R), BF16),
            pltpu.VMEM((LEAFS, PROBES, R), BF16),
            pltpu.VMEM((SUBS, PROBES // 2, 2 * R), F32),
            pltpu.VMEM((SUBS, PROBES // 2, 2 * R), F32),
            pltpu.VMEM((TOPS, PROBES // 2, 2 * R), F32),
            pltpu.VMEM((TOPS, PROBES // 2, 2 * R), F32),
            dma((6,)),
            dma((CHUNKS + 1,)),
            dma((2, CHUNKS, 2)),
            dma((2, CHUNKS, 2)),
            dma((4, 2)),
            dma((4, 2)),
            dma((2, 3)),
            dma((2, 3)),
            dma((2, 7)),
            dma((2, 7)),
            dma((2, 3)),
            dma((2, 3)),
        ],
        compiler_params=pltpu.CompilerParams(
            collective_id=0, has_side_effects=True, vmem_limit_bytes=56 << 20
        ),
        cost_estimate=pl.CostEstimate(
            flops=6_000_000_000, bytes_accessed=6_000_000, transcendentals=17_000_000
        ),
    )(*arguments)


def solution(mesh):
    split_over_both = P(("leaf", "sub"), None, None)
    in_specs = (
        split_over_both,
        split_over_both,
        split_over_both,
        split_over_both,
        split_over_both,
        split_over_both,
        P(),
        P(("leaf", "sub"), None),
        P(("leaf", "sub"), None),
        P("leaf", None),
        P(),
        P(),
        P(),
    )
    return jax.shard_map(
        on_device,
        mesh=mesh,
        in_specs=in_specs,
        out_specs=(split_over_both, split_over_both),
        check_vma=False,
    )
```

time: 524 us -> 107 us (0.20)
  waiting for transfers between devices: 197 us -> 0 us
  other arithmetic: 143 us -> 0 us
  Pallas kernels: 0 us -> 99.7 us
  matrix products: 87.6 us -> 0 us
  starting transfers between devices: 39.2 us -> 0 us
  local copies, waits for them, and re-layouts: 40.1 us -> 5.12 us
  between operations: 16.5 us -> 1.93 us
    psum x2 -> x0, waiting for transfers between devices: 197 us -> none  [on_device(): all_top = lax.psum(slots, ('leaf', 'sub'))]
    dot_general x2 -> x0, other arithmetic: 131 us -> none  [on_device(): jnp.einsum('iknm,ikpm->ipn', near_blocks, wide_vector[near_local], prefer...]
    pallas_call x0 -> x1, Pallas kernels: none -> 99.7 us  [on_device(): pl.pallas_call(kernel, out_shape=(result, result), in_specs=[hbm] * 6 + [...]
    dot_general x18 -> x0, matrix products: 87.6 us -> none  [the longest x2 27.7 us: on_device(): jnp.einsum('iknm,ikpm->ipn', near_blocks, wide_vector[near_local], prefer...]
    ppermute x12 -> x0, starting transfers between devices: 39.1 us -> none  [the longest x6 25.9 us: padded(): lax.ppermute(lax.slice_in_dim(block, 0, width, axis=dim), axis, backward)]
    gather x9 -> x0, local copies, waits for them, and re-layouts: 21.2 us -> none  [the longest x2 9.3 us: on_device(): wide_vector[near_local]]
    slice x6 -> x0, local copies, waits for them, and re-layouts: 11.4 us -> none  [the longest x3 9.23 us: matern(): right_side[..., feature, None, :]]
    concatenate x6 -> x0, other arithmetic: 8.1 us -> none  [padded(): block = jnp.concatenate([low, block, high], axis=dim)]
  transfers between devices with their start and end apart: 14 -> 0, of which waited for: 2 -> 0; matrix products, arithmetic and copies ran while one was open for 42% -> 0% of each run, Pallas kernels for 0% -> 0%
where the time goes in v1:
time: 107 us
  Pallas kernels  99.7 us (93%)
  local copies, waits for them, and re-layouts  5.12 us (5%)
  between operations  1.93 us (2%)
    pallas_call x1, Pallas kernels, on_device(): pl.pallas_call(kernel, out_shape=(result, result), in_specs=[hbm] * 6 + [...  99.7 us
    unnamed x3, local copies, waits for them, and re-layouts  5.12 us

profile of v1, /device:TPU:1, one launch (start us, length us, event | category | flops | bytes accessed | tf_op | source)
XLA Modules:
  0.0 106.8 jit_solution(9546511070155632767)
XLA Ops:
  1.9 1.4 %copy.15.near_list = s32[64,8]{1,0:T(8,128)} copy(s32[64,8]{0,1:T(8,128)} %param.20) | data formatting | bytes 4096 | tf_op args[7]
  3.3 99.7 %shard_map.140 = (bf16[64,32,128]{2,1,0:T(8,128)(2,1)}, bf16[64,32,128]{2,1,0:T(8,128)(2,1)}) custom-call(f32[64,8,128]{2,1,0:T(8,128)} %points_ref.1, bf16[64,32,128]{2,1,0:T(8,128)(2,1)} %probes_ref.1, bf16[64,64,128]{2,1,0:T(8,128)(2,1)} %basis_ref.1, f32[64,64,64]{2,1,0:T(8,128)} %transfer_ref.1, f32[8,64,64]{2,1,0:T(8,128)} %top_transfer_ref.1, ...), custom_call_target="tpu_custom_call" | custom-call | flops 6000000000 | bytes 6000000 | tf_op jit(solution)/shard_map/pallas_call | solution.py:503
  103.1 1.9 %copy.20 = bf16[64,32,128]{2,1,0:T(8,128)(2,1)} copy(bf16[64,32,128]{2,1,0:T(8,128)(2,1)} %get-tuple-element.4) | data formatting | bytes 1048576
  104.9 1.9 %copy.21 = bf16[64,32,128]{2,1,0:T(8,128)(2,1)} copy(bf16[64,32,128]{2,1,0:T(8,128)(2,1)} %get-tuple-element.5) | data formatting | bytes 1048576

commit v2 on v1

--- a/solution.py
+++ b/solution.py
@@ -112,7 +112,7 @@
     top_transfer_ref,
     mid_skeleton_ref,
     top_skeleton_ref,
-    near_list,
+    near_list_ref,
     mid_list,
     top_list,
     inv_scale,
@@ -135,19 +135,19 @@
     left_v,
     right_v,
     blocks,
+    distance_v,
     mid_left,
-    coupling_h,
-    coupling_l,
-    top_coupling_h,
-    top_coupling_l,
+    mid_coupling,
+    top_coupling,
     mids_0,
     mids_1,
-    mid_both,
-    leaf_total,
+    mid_total,
+    part,
     sums_0,
     sums_1,
     tops_0,
     tops_1,
+    near_list,
     local_sem,
     out_sem,
     bulk_send,
@@ -156,24 +156,19 @@
     side_recv,
     sub_send,
     sub_recv,
-    near_send,
-    near_recv,
-    far_send,
-    far_recv,
+    top_send,
+    top_recv,
 ):
     leaf = lax.axis_index("leaf")
     sub = lax.axis_index("sub")
     position = leaf * SUBS + sub
-    plane = lax.div(leaf, 8)
-    place = lax.rem(leaf, 8)
     before = device_at(position - 1)
     after = device_at(position + 1)
     sub_ids = [(leaf, lax.rem(sub + k, SUBS)) for k in range(1, SUBS)]
-    near_ids = [(plane * 8 + lax.rem(place + k, 8), sub) for k in range(1, 8)]
-    far_ids = [(lax.rem(leaf + 8 * k, TOPS), sub) for k in range(1, 4)]
+    top_ids = [(lax.rem(leaf + k, TOPS), sub) for k in range(1, TOPS)]
 
     barrier = pltpu.get_barrier_semaphore()
-    partners = [before, after, *sub_ids, *near_ids, *far_ids]
+    partners = [before, after, *sub_ids, *top_ids]
     for partner in partners:
         pl.semaphore_signal(barrier, inc=1, device_id=partner, device_id_type=MESH)
 
@@ -188,6 +183,7 @@
                 (top_transfer_ref, top_v),
                 (points_ref, points_v.at[own]),
                 (mid_skeleton_ref, skeleton.at[pl.ds(MIDS, MIDS)]),
+                (near_list_ref, near_list),
             )
         )
     ]
@@ -260,20 +256,27 @@
     for m in range(MIDS):
         top_h[m], top_l[m] = split(top_v[m])
 
+    lane = lax.broadcasted_iota(jnp.int32, (PROBES, 2 * R), 1)
+    lower = lane < R
+
     def upward(vector, mids, sums):
         def step(m, partial):
-            total = jnp.zeros((PROBES, R), F32)
-            for c in range(GROUP):
+            parts = []
+            for c in range(0, GROUP, 2):
                 leaf_id = m * GROUP + c
-                coef = nt(vector[LEAFS + leaf_id], basis[leaf_id])
-                total += wide_product(stacked(coef), transfer_h[leaf_id], transfer_l[leaf_id], nn)
-            mids[MIDS + m] = pack(total)
-            both = stacked(total)
-            mid_both[MIDS + m] = both
-            return partial + wide_product(both, top_h[m], top_l[m], nn)
-
-        partial = lax.fori_loop(0, MIDS, step, jnp.zeros((PROBES, R), F32))
-        sums[sub] = pack(partial)
+                pair = vector[pl.ds(LEAFS + leaf_id, 2)].reshape(2 * PROBES, POINTS)
+                coef = nt(pair, basis[pl.ds(leaf_id, 2)].reshape(2 * R, POINTS))
+                parts.append(jnp.where(lower, coef[:PROBES], coef[PROBES:]))
+            total = wide_product(
+                stacked(jnp.concatenate(parts, axis=1)),
+                transfer_h[pl.ds(m * GROUP, GROUP)].reshape(GROUP * R, R),
+                transfer_l[pl.ds(m * GROUP, GROUP)].reshape(GROUP * R, R),
+                nn,
+            )
+            mids[MIDS + m] = jnp.concatenate([total, total], axis=1).astype(BF16)
+            return partial + wide_product(stacked(total), top_h[m], top_l[m], nn)
+
+        sums[sub] = pack(lax.fori_loop(0, MIDS, step, jnp.zeros((PROBES, R), F32), unroll=2))
 
     def small_copies(turn, mids, sums, tops):
         sides = halo(mids, MIDS, mids, 0, MIDS, MIDS, side_send.at[2 + turn], side_recv.at[2 + turn])
@@ -281,20 +284,11 @@
             remote(sums.at[sub], sums.at[sub], sub_send.at[turn, k], sub_recv.at[turn, k], device)
             for k, device in enumerate(sub_ids)
         ]
-        in_plane = [
-            remote(
-                tops.at[leaf], tops.at[leaf], near_send.at[turn, k], near_recv.at[turn, k], device
-            )
-            for k, device in enumerate(near_ids)
+        over_tops = [
+            remote(tops.at[leaf], tops.at[leaf], top_send.at[turn, k], top_recv.at[turn, k], device)
+            for k, device in enumerate(top_ids)
         ]
-        rows = pl.ds(plane * 8, 8)
-        over_planes = [
-            remote(
-                tops.at[rows], tops.at[rows], far_send.at[turn, k], far_recv.at[turn, k], device
-            )
-            for k, device in enumerate(far_ids)
-        ]
-        return sides, in_sub, in_plane, over_planes
+        return sides, in_sub, over_tops
 
     def begin(copies):
         for copy in copies:
@@ -308,63 +302,62 @@
         total = sums[0]
         for k in range(1, SUBS):
             total += sums[k]
-        tops[leaf] = total
+        tops[leaf] = total.astype(BF16)
 
     def mid_target(m, e):
         listed = mid_list[m, e]
         target = listed - position * MIDS + MIDS
         return listed, jnp.clip(target, 0, 3 * MIDS - 1)
 
-    def downward(mids, tops):
-        def take(m, carry):
-            mid_both[m] = stacked(unpack(mids[m]))
+    def downward(mids, tops, use):
+        parts = []
+        for e in range(TOP_NEAR):
+            both = unpack(tops[jnp.clip(top_list[0, e], 0, TOPS - 1)].astype(F32))
+            parts.append(jnp.concatenate([both, both], axis=1).astype(BF16))
+        top_both = stacked(nn(jnp.concatenate(parts, axis=1), top_coupling[...]))
+
+        def total_step(m, carry):
+            total = wide_product(top_both, top_h[m], top_l[m], nt)
+            near = jnp.concatenate([mids[mid_target(m, e)[1]] for e in range(MID_NEAR)], axis=1)
+            mid_total[m] = stacked(total + nn(near, mid_coupling[m]))
             return carry
 
-        lax.fori_loop(0, MIDS, take, 0)
-        lax.fori_loop(2 * MIDS, 3 * MIDS, take, 0)
-        top_local = jnp.zeros((PROBES, R), F32)
-        for e in range(TOP_NEAR):
-            target = jnp.clip(top_list[0, e], 0, TOPS - 1)
-            top_local += wide_product(
-                stacked(unpack(tops[target])), top_coupling_h[e], top_coupling_l[e], nn
+        lax.fori_loop(0, MIDS, total_step, 0, unroll=4)
+
+        def step(m, carry):
+            totals = wide_product(
+                mid_total[m],
+                transfer_h[pl.ds(m * GROUP, GROUP)].reshape(GROUP * R, R),
+                transfer_l[pl.ds(m * GROUP, GROUP)].reshape(GROUP * R, R),
+                nt,
             )
-        top_both = stacked(top_local)
-
-        def step(m, carry):
-            total = wide_product(top_both, top_h[m], top_l[m], nt)
-            for e in range(MID_NEAR):
-                _, target = mid_target(m, e)
-                total += wide_product(mid_both[target], coupling_h[m, e], coupling_l[m, e], nn)
-            both = stacked(total)
-            for c in range(GROUP):
+            for c in range(0, GROUP, 2):
                 leaf_id = m * GROUP + c
-                leaf_total[leaf_id] = wide_product(
-                    both, transfer_h[leaf_id], transfer_l[leaf_id], nt
+                pair = totals[:, c * R : (c + 2) * R]
+                pair = jnp.concatenate(
+                    [jnp.where(lower, pair, 0.0), jnp.where(lower, 0.0, pair)], axis=0
                 ).astype(BF16)
+                far = nn(pair, basis[pl.ds(leaf_id, 2)].reshape(2 * R, POINTS))
+                use(leaf_id, far.reshape(2, PROBES, POINTS))
             return carry
 
-        lax.fori_loop(0, MIDS, step, 0)
+        lax.fori_loop(0, MIDS, step, 0, unroll=2)
 
     def near_target(i, e):
-        listed = near_list[i, e]
+        listed = near_list[e, i]
         target = listed - position * LEAFS + LEAFS
         return listed, jnp.clip(target, 0, 3 * LEAFS - 1)
 
-    def products(vector, result, offset, first, count):
+    def near_products(vector, first, count, use):
         def step(i, carry):
-            parts = []
-            for e in range(NEAR):
-                _, target = near_target(i, e)
-                parts.append(vector[target])
+            parts = [vector[near_target(i, e)[1]] for e in range(NEAR)]
             total = nn(jnp.concatenate(parts, axis=1), blocks[i])
-            total += nn(leaf_total[i], basis[i])
-            total += noise * vector[LEAFS + i].astype(F32)
-            result[offset + i] = total.astype(BF16)
+            use(i, total + noise * vector[LEAFS + i].astype(F32))
             return carry
 
-        lax.fori_loop(first, first + count, step, 0, unroll=2)
-
-    sides, in_sub, in_plane, over_planes = small_copies(0, mids_0, sums_0, tops_0)
+        lax.fori_loop(first, first + count, step, 0, unroll=8)
+
+    sides, in_sub, over_tops = small_copies(0, mids_0, sums_0, tops_0)
     upward(vector_0, mids_0, sums_0)
     begin(in_sub)
     begin(sides)
@@ -372,6 +365,7 @@
         begin(probes_halo[k])
 
     loads[4].wait()
+    loads[6].wait()
 
     def own_features(i, carry):
         left, right = features(points_v[LEAFS + i] * scales, True, True)
@@ -383,40 +377,20 @@
 
     small_scales = scales[:, :R]
     (top_right,) = features(top_skeleton_ref[leaf] * small_scales, False, True)
+    top_right = top_right.astype(BF16)
     for e in range(TOP_NEAR):
         target = top_list[0, e]
         (top_left,) = features(
             top_skeleton_ref[jnp.clip(target, 0, TOPS - 1)] * small_scales, True, False
         )
-        squared = nn(top_left.T.astype(BF16), top_right.astype(BF16))
-        value = matern(squared, jnp.where(target >= 0, amp, 0.0))
-        top_coupling_h[e], top_coupling_l[e] = split(value)
+        value = matern(
+            nn(top_left.T.astype(BF16), top_right), jnp.where(target >= 0, amp, 0.0)
+        )
+        top_coupling[pl.ds(e * POINTS, POINTS)] = stacked(value)
 
     finish(in_sub)
     sum_tops(sums_0, tops_0)
-    begin(in_plane)
-
-    finish(points_halo)
-
-    def halo_features(i, carry):
-        (left,) = features(points_v[i] * scales, True, False)
-        left_v[i] = left.T.astype(BF16)
-        return carry
-
-    lax.fori_loop(0, LEAFS, halo_features, 0, unroll=2)
-    lax.fori_loop(2 * LEAFS, 3 * LEAFS, halo_features, 0, unroll=2)
-    finish(in_plane)
-    begin(over_planes)
-
-    def near_blocks(i, carry):
-        right = right_v[i]
-        for e in range(NEAR):
-            listed, target = near_target(i, e)
-            value = matern(nn(left_v[target], right), jnp.where(listed >= 0, amp, 0.0))
-            blocks[i, pl.ds(e * POINTS, POINTS)] = value.astype(BF16)
-        return carry
-
-    lax.fori_loop(0, LEAFS, near_blocks, 0)
+    begin(over_tops)
 
     loads[5].wait()
     finish(skeleton_halo)
@@ -426,7 +400,7 @@
         mid_left[m] = left.T.astype(BF16)
         return carry
 
-    lax.fori_loop(0, 3 * MIDS, mid_features, 0)
+    lax.fori_loop(0, 3 * MIDS, mid_features, 0, unroll=2)
 
     def mid_couplings(m, carry):
         (right,) = features(skeleton[MIDS + m] * small_scales, False, True)
@@ -434,14 +408,47 @@
         for e in range(MID_NEAR):
             listed, target = mid_target(m, e)
             value = matern(nn(mid_left[target], right), jnp.where(listed >= 0, amp, 0.0))
-            coupling_h[m, e], coupling_l[m, e] = split(value)
+            mid_coupling[m, pl.ds(e * POINTS, POINTS)] = stacked(value)
         return carry
 
     lax.fori_loop(0, MIDS, mid_couplings, 0)
 
-    finish(over_planes)
+    finish(points_halo)
+
+    def halo_features(i, carry):
+        (left,) = features(points_v[i] * scales, True, False)
+        left_v[i] = left.T.astype(BF16)
+        return carry
+
+    lax.fori_loop(0, LEAFS, halo_features, 0, unroll=4)
+    lax.fori_loop(2 * LEAFS, 3 * LEAFS, halo_features, 0, unroll=4)
+
+    def distances(i, h, e):
+        distance_v[h, e] = nn(left_v[near_target(i, e)[1]], right_v[i])
+
+    for h in range(2):
+        for e in range(NEAR):
+            distances(h, h, e)
+
+    def near_blocks(k, carry):
+        for e in range(NEAR):
+            for h in range(2):
+                i = 2 * k + h
+                scale = jnp.where(near_list[e, i] >= 0, amp, 0.0)
+                value = matern(distance_v[h, e], scale)
+                blocks[i, pl.ds(e * POINTS, POINTS)] = value.astype(BF16)
+                distances(jnp.minimum(i + 2, LEAFS - 1), h, e)
+        return carry
+
+    lax.fori_loop(0, LEAFS // 2, near_blocks, 0)
+
+    finish(over_tops)
     finish(sides)
-    downward(mids_0, tops_0)
+
+    def keep_far(i, far):
+        part[pl.ds(i, 2)] = far
+
+    downward(mids_0, tops_0, keep_far)
     for chunk in probes_halo:
         finish(chunk)
 
@@ -458,39 +465,62 @@
         )
         for k in range(CHUNKS)
     ]
-    sides, in_sub, in_plane, over_planes = small_copies(1, mids_1, sums_1, tops_1)
+
+    def finish_first(i, near):
+        vector_1[LEAFS + i] = (near + part[i]).astype(BF16)
+
     for k in range(CHUNKS):
-        products(vector_0, vector_1, LEAFS, k * per_chunk, per_chunk)
-        if k < CHUNKS // 2:
+        near_products(vector_0, k * per_chunk, per_chunk, finish_first)
+        if k < CHUNKS - 1:
             begin(first_halo[k])
+    sides, in_sub, over_tops = small_copies(1, mids_1, sums_1, tops_1)
     upward(vector_1, mids_1, sums_1)
     begin(in_sub)
     begin(sides)
-    for k in range(CHUNKS // 2, CHUNKS):
-        begin(first_halo[k])
+    begin(first_halo[CHUNKS - 1])
     first_out = pltpu.make_async_copy(vector_1.at[own], first_ref, out_sem.at[CHUNKS])
     first_out.start()
 
     finish(in_sub)
     sum_tops(sums_1, tops_1)
-    begin(in_plane)
-    finish(in_plane)
-    begin(over_planes)
-    finish(over_planes)
-    finish(sides)
-    downward(mids_1, tops_1)
+    begin(over_tops)
     for chunk in first_halo:
         finish(chunk)
-    outs = []
-    for k in range(CHUNKS):
-        rows = pl.ds(k * per_chunk, per_chunk)
-        products(vector_1, result_v, 0, k * per_chunk, per_chunk)
-        out = pltpu.make_async_copy(result_v.at[rows], second_ref.at[rows], out_sem.at[k])
-        out.start()
-        outs.append(out)
-    for out in outs:
-        out.wait()
+
+    def keep_near(i, near):
+        part[i] = near
+
+    near_products(vector_1, 0, LEAFS, keep_near)
+    finish(over_tops)
+    finish(sides)
+
+    def finish_second(i, far):
+        result_v[pl.ds(i, 2)] = (far + part[pl.ds(i, 2)]).astype(BF16)
+
+    downward(mids_1, tops_1, finish_second)
+    second_out = pltpu.make_async_copy(result_v, second_ref, out_sem.at[0])
+    second_out.start()
+    second_out.wait()
     first_out.wait()
+
+
+def copy_out(first_ref, second_ref, first_out, second_out, held, in_sem, out_sem):
+    rows = LEAFS // CHUNKS
+    into, out = [], []
+    for p, (source, target) in enumerate(((first_ref, first_out), (second_ref, second_out))):
+        for k in range(CHUNKS):
+            some = pl.ds(k * rows, rows)
+            into.append(
+                pltpu.make_async_copy(source.at[some], held.at[p, some], in_sem.at[p, k])
+            )
+            out.append(pltpu.make_async_copy(held.at[p, some], target.at[some], out_sem.at[p, k]))
+    for copy in into:
+        copy.start()
+    for k, copy in enumerate(out):
+        into[k].wait()
+        copy.start()
+    for copy in out:
+        copy.wait()
 
 
 def on_device(*arguments):
@@ -500,10 +530,10 @@
     dma = pltpu.SemaphoreType.DMA
     wide = (3 * LEAFS, PROBES, POINTS)
     result = jax.ShapeDtypeStruct((LEAFS, PROBES, POINTS), BF16)
-    return pl.pallas_call(
+    products = pl.pallas_call(
         kernel,
         out_shape=(result, result),
-        in_specs=[hbm] * 6 + [vmem] + [smem] * 6,
+        in_specs=[hbm] * 6 + [vmem, hbm] + [smem] * 5,
         out_specs=(hbm, hbm),
         scratch_shapes=[
             pltpu.VMEM((3 * LEAFS, 8, POINTS), F32),
@@ -521,20 +551,20 @@
             pltpu.VMEM((3 * LEAFS, POINTS, R), BF16),
             pltpu.VMEM((LEAFS, R, POINTS), BF16),
             pltpu.VMEM((LEAFS, NEAR * POINTS, POINTS), BF16),
+            pltpu.VMEM((2, NEAR, POINTS, POINTS), F32),
             pltpu.VMEM((3 * MIDS, R, R), BF16),
-            pltpu.VMEM((MIDS, MID_NEAR, R, R), BF16),
-            pltpu.VMEM((MIDS, MID_NEAR, R, R), BF16),
-            pltpu.VMEM((TOP_NEAR, R, R), BF16),
-            pltpu.VMEM((TOP_NEAR, R, R), BF16),
-            pltpu.VMEM((3 * MIDS, PROBES // 2, 2 * R), F32),
-            pltpu.VMEM((3 * MIDS, PROBES // 2, 2 * R), F32),
-            pltpu.VMEM((3 * MIDS, 2 * PROBES, R), BF16),
-            pltpu.VMEM((LEAFS, PROBES, R), BF16),
+            pltpu.VMEM((MIDS, MID_NEAR * 2 * R, R), BF16),
+            pltpu.VMEM((TOP_NEAR * 2 * R, R), BF16),
+            pltpu.VMEM((3 * MIDS, PROBES, 2 * R), BF16),
+            pltpu.VMEM((3 * MIDS, PROBES, 2 * R), BF16),
+            pltpu.VMEM((MIDS, 2 * PROBES, R), BF16),
+            pltpu.VMEM((LEAFS, PROBES, POINTS), F32),
             pltpu.VMEM((SUBS, PROBES // 2, 2 * R), F32),
             pltpu.VMEM((SUBS, PROBES // 2, 2 * R), F32),
-            pltpu.VMEM((TOPS, PROBES // 2, 2 * R), F32),
-            pltpu.VMEM((TOPS, PROBES // 2, 2 * R), F32),
-            dma((6,)),
+            pltpu.VMEM((TOPS, PROBES // 2, 2 * R), BF16),
+            pltpu.VMEM((TOPS, PROBES // 2, 2 * R), BF16),
+            pltpu.SMEM((NEAR, LEAFS), jnp.int32),
+            dma((7,)),
             dma((CHUNKS + 1,)),
             dma((2, CHUNKS, 2)),
             dma((2, CHUNKS, 2)),
@@ -542,10 +572,8 @@
             dma((4, 2)),
             dma((2, 3)),
             dma((2, 3)),
-            dma((2, 7)),
-            dma((2, 7)),
-            dma((2, 3)),
-            dma((2, 3)),
+            dma((2, TOPS - 1)),
+            dma((2, TOPS - 1)),
         ],
         compiler_params=pltpu.CompilerParams(
             collective_id=0, has_side_effects=True, vmem_limit_bytes=56 << 20
@@ -553,7 +581,18 @@
         cost_estimate=pl.CostEstimate(
             flops=6_000_000_000, bytes_accessed=6_000_000, transcendentals=17_000_000
         ),
-    )(*arguments)
+    )(*arguments[:7], arguments[7].T, *arguments[8:])
+    return pl.pallas_call(
+        copy_out,
+        out_shape=(result, result),
+        in_specs=[hbm, hbm],
+        out_specs=(hbm, hbm),
+        scratch_shapes=[
+            pltpu.VMEM((2, LEAFS, PROBES, POINTS), BF16),
+            dma((2, CHUNKS)),
+            dma((2, CHUNKS)),
+        ],
+    )(*products)
 
 
 def solution(mesh):

time: 107 us -> 77.9 us (0.73)
  Pallas kernels: 99.7 us -> 75.8 us
  local copies, waits for them, and re-layouts: 5.12 us -> 0 us
    pallas_call x1, Pallas kernels: 99.7 us -> 73.7 us  [on_device(): pl.pallas_call(kernel, out_shape=(result, result), in_specs=[hbm] * 6 + [...]
    unnamed x3 -> x0, local copies, waits for them, and re-layouts: 5.12 us -> none
    pallas_call x0 -> x1, Pallas kernels: none -> 2.09 us  [on_device(): pl.pallas_call(copy_out, out_shape=(result, result), in_specs=[hbm, hbm],...]
where the time goes in v2:
time: 77.9 us; the launch traced here: 77.7 us
  Pallas kernels  75.8 us (97%)
  between operations  1.93 us (2%)
    pallas_call x1, Pallas kernels, on_device(): pl.pallas_call(kernel, out_shape=(result, result), in_specs=[hbm] * 6 + [...  73.7 us
    pallas_call x1, Pallas kernels, on_device(): pl.pallas_call(copy_out, out_shape=(result, result), in_specs=[hbm, hbm],...  2.09 us

profile of v2, /device:TPU:1, one launch (start us, length us, event | category | flops | bytes accessed | tf_op | source)
XLA Modules:
  0.0 77.7 jit_solution(3652549402968112252)
XLA Ops:
  1.9 73.7 %shard_map.140 = (bf16[64,32,128]{2,1,0:T(8,128)(2,1)}, bf16[64,32,128]{2,1,0:T(8,128)(2,1)}) custom-call(f32[64,8,128]{2,1,0:T(8,128)} %points_ref.1, bf16[64,32,128]{2,1,0:T(8,128)(2,1)} %probes_ref.1, bf16[64,64,128]{2,1,0:T(8,128)(2,1)} %basis_ref.1, f32[64,64,64]{2,1,0:T(8,128)} %transfer_ref.1, f32[8,64,64]{2,1,0:T(8,128)} %top_transfer_ref.1, ...), custom_call_target="tpu_custom_call" | custom-call | flops 6000000000 | bytes 6000000 | tf_op jit(solution)/shard_map/pallas_call | solution.py:533
  75.6 2.1 %shard_map.141 = (bf16[64,32,128]{2,1,0:T(8,128)(2,1)}, bf16[64,32,128]{2,1,0:T(8,128)(2,1)}) custom-call(bf16[64,32,128]{2,1,0:T(8,128)(2,1)} %get-tuple-element.4.first_ref, bf16[64,32,128]{2,1,0:T(8,128)(2,1)} %get-tuple-element.5.second_ref), custom_call_target="tpu_custom_call" | custom-call | tf_op jit(solution)/shard_map/pallas_call | solution.py:585

commit v3 on v2

--- a/solution.py
+++ b/solution.py
@@ -234,7 +234,7 @@
         )
         for k in range(CHUNKS)
     ]
-    for copy in [*points_halo, *skeleton_halo, *probes_halo[0], *probes_halo[1]]:
+    for copy in [*points_halo, *skeleton_halo]:
         copy.start()
 
     row = lax.broadcasted_iota(jnp.int32, (8, POINTS), 0)
@@ -361,8 +361,9 @@
     upward(vector_0, mids_0, sums_0)
     begin(in_sub)
     begin(sides)
-    for k in range(2, CHUNKS):
-        begin(probes_halo[k])
+
+    for chunk in probes_halo:
+        begin(chunk)
 
     loads[4].wait()
     loads[6].wait()
@@ -388,31 +389,6 @@
         )
         top_coupling[pl.ds(e * POINTS, POINTS)] = stacked(value)
 
-    finish(in_sub)
-    sum_tops(sums_0, tops_0)
-    begin(over_tops)
-
-    loads[5].wait()
-    finish(skeleton_halo)
-
-    def mid_features(m, carry):
-        (left,) = features(skeleton[m] * small_scales, True, False)
-        mid_left[m] = left.T.astype(BF16)
-        return carry
-
-    lax.fori_loop(0, 3 * MIDS, mid_features, 0, unroll=2)
-
-    def mid_couplings(m, carry):
-        (right,) = features(skeleton[MIDS + m] * small_scales, False, True)
-        right = right.astype(BF16)
-        for e in range(MID_NEAR):
-            listed, target = mid_target(m, e)
-            value = matern(nn(mid_left[target], right), jnp.where(listed >= 0, amp, 0.0))
-            mid_coupling[m, pl.ds(e * POINTS, POINTS)] = stacked(value)
-        return carry
-
-    lax.fori_loop(0, MIDS, mid_couplings, 0)
-
     finish(points_halo)
 
     def halo_features(i, carry):
@@ -422,6 +398,10 @@
 
     lax.fori_loop(0, LEAFS, halo_features, 0, unroll=4)
     lax.fori_loop(2 * LEAFS, 3 * LEAFS, halo_features, 0, unroll=4)
+
+    finish(in_sub)
+    sum_tops(sums_0, tops_0)
+    begin(over_tops)
 
     def distances(i, h, e):
         distance_v[h, e] = nn(left_v[near_target(i, e)[1]], right_v[i])
@@ -441,6 +421,27 @@
         return carry
 
     lax.fori_loop(0, LEAFS // 2, near_blocks, 0)
+
+    loads[5].wait()
+    finish(skeleton_halo)
+
+    def mid_features(m, carry):
+        (left,) = features(skeleton[m] * small_scales, True, False)
+        mid_left[m] = left.T.astype(BF16)
+        return carry
+
+    lax.fori_loop(0, 3 * MIDS, mid_features, 0, unroll=2)
+
+    def mid_couplings(m, carry):
+        (right,) = features(skeleton[MIDS + m] * small_scales, False, True)
+        right = right.astype(BF16)
+        for e in range(MID_NEAR):
+            listed, target = mid_target(m, e)
+            value = matern(nn(mid_left[target], right), jnp.where(listed >= 0, amp, 0.0))
+            mid_coupling[m, pl.ds(e * POINTS, POINTS)] = stacked(value)
+        return carry
+
+    lax.fori_loop(0, MIDS, mid_couplings, 0)
 
     finish(over_tops)
     finish(sides)
@@ -471,13 +472,11 @@
 
     for k in range(CHUNKS):
         near_products(vector_0, k * per_chunk, per_chunk, finish_first)
-        if k < CHUNKS - 1:
-            begin(first_halo[k])
+        begin(first_halo[k])
     sides, in_sub, over_tops = small_copies(1, mids_1, sums_1, tops_1)
     upward(vector_1, mids_1, sums_1)
     begin(in_sub)
     begin(sides)
-    begin(first_halo[CHUNKS - 1])
     first_out = pltpu.make_async_copy(vector_1.at[own], first_ref, out_sem.at[CHUNKS])
     first_out.start()
 

time: 77.9 us -> 72.5 us (0.931)
  Pallas kernels: 75.8 us -> 70.4 us
    pallas_call x1, Pallas kernels: 73.7 us -> 68.3 us  [on_device(): pl.pallas_call(kernel, out_shape=(result, result), in_specs=[hbm] * 6 + [...]
where the time goes in v3:
time: 72.5 us; the launch traced here: 72.4 us
  Pallas kernels  70.4 us (97%)
  between operations  1.93 us (3%)
    pallas_call x1, Pallas kernels, on_device(): pl.pallas_call(kernel, out_shape=(result, result), in_specs=[hbm] * 6 + [...  68.3 us
    pallas_call x1, Pallas kernels, on_device(): pl.pallas_call(copy_out, out_shape=(result, result), in_specs=[hbm, hbm],...  2.09 us

profile of v3, /device:TPU:1, one launch (start us, length us, event | category | flops | bytes accessed | tf_op | source)
XLA Modules:
  0.0 72.4 jit_solution(14430919989414249538)
XLA Ops:
  1.9 68.3 %shard_map.140 = (bf16[64,32,128]{2,1,0:T(8,128)(2,1)}, bf16[64,32,128]{2,1,0:T(8,128)(2,1)}) custom-call(f32[64,8,128]{2,1,0:T(8,128)} %points_ref.1, bf16[64,32,128]{2,1,0:T(8,128)(2,1)} %probes_ref.1, bf16[64,64,128]{2,1,0:T(8,128)(2,1)} %basis_ref.1, f32[64,64,64]{2,1,0:T(8,128)} %transfer_ref.1, f32[8,64,64]{2,1,0:T(8,128)} %top_transfer_ref.1, ...), custom_call_target="tpu_custom_call" | custom-call | flops 6000000000 | bytes 6000000 | tf_op jit(solution)/shard_map/pallas_call | solution.py:532
  70.3 2.1 %shard_map.141 = (bf16[64,32,128]{2,1,0:T(8,128)(2,1)}, bf16[64,32,128]{2,1,0:T(8,128)(2,1)}) custom-call(bf16[64,32,128]{2,1,0:T(8,128)(2,1)} %get-tuple-element.4.first_ref, bf16[64,32,128]{2,1,0:T(8,128)(2,1)} %get-tuple-element.5.second_ref), custom_call_target="tpu_custom_call" | custom-call | tf_op jit(solution)/shard_map/pallas_call | solution.py:584
